TPU v7x, 512 devices: a whole 4x8x8 slice. The times are simulated.
512 devices in a mesh: sub: 128 (over x, z_lo, y, core), mode: 4 (over z_hi).
Axes of the slice: x: 4, y: 8, z: 8 (z_hi: 4, z_lo: 2; z = z_hi * 2 + z_lo), core: 2. Of those that a mesh axis runs over, the one named last changes fastest.
Arguments:
- leaf_coords: bfloat16 [1024, 768, 128], P('sub', 'mode'), may hold values from -6 to 6
- leaf_modes: bfloat16 [1024, 128, 512], P('sub'), may hold values from -0.5 to 0.5
- constraint_modes: bfloat16 [1024, 3, 256, 512], P('sub'), may hold values from -0.375 to 0.375
- sep_one: bfloat16 [768, 16384], P('mode', 'sub'), may hold values from -6 to 6
- sep_two: bfloat16 [768, 8192], P('mode', 'sub'), may hold values from -6 to 6
- sep_three: bfloat16 [768, 4096], P('mode', 'sub'), may hold values from -6 to 6
- cluster_rows: int32 [384, 512], P('sub'), may hold values from 0 to 524287, as said below
- operators: bfloat16 [384, 512, 384], P('sub'), may hold values from -0.25 to 0.25
- compliance: float32 [384, 384], P('sub'), may hold values from 0.05 to 0.5
- modal_weight: float32 [768], P('mode'), may hold values from 0.5 to 2
Outputs:
- stresses: float32 [384, 768, 384], P('sub', 'mode')
- strain_energy: float32 [24576], P(('sub', 'mode'))
Inputs may be any that keep to these rules, and one draw needn't show every extreme that they name: cluster_rows[c, j] = s * 4096 + r names column r of the displacement columns of the leaves of sub index s (its leaves laid end to end). The clusters of sub index d read only from sub indices d - 2 to d + 2 taken around the axis, and at most 384 of their 1536 rows from any one of these indices; that most is reached for every d from one of the five.
All inputs are finite; a program needn't handle non-finite values.
Results may differ from a plain program's by a relative error of at most 0.0029.
Values may be sent and summed in bfloat16 or wider, within the bound.
A program may use at most 64 MiB of HBM per device.

v0:
```python
import jax
import jax.numpy as jnp
from jax import lax
from jax.sharding import PartitionSpec as P

M = 768


def from_partner(value, axis, bit):
    mask = 2**bit
    pairs = [(source, source ^ mask) for source in range(lax.axis_size(axis))]
    return lax.ppermute(value, axis, pairs)


def passed_along(shard, axis, by):
    peers = lax.axis_size(axis)
    return lax.ppermute(shard, axis, [(i, (i + by) % peers) for i in range(peers)])


def in_blocks(shard, dim, peers):
    before, after = (shard.shape[:dim], shard.shape[dim + 1 :])
    return jnp.moveaxis(shard.reshape(*before, peers, -1, *after), dim, 0)


def sum_at_owner(shard, axis, dim):
    peers = lax.axis_size(axis)
    parts = lax.all_to_all(in_blocks(shard, dim, peers), axis, 0, 0, tiled=True)
    return jnp.sum(parts, axis=0)


def join_halves(mine, partner, upper_half):
    return jnp.where(
        upper_half,
        jnp.concatenate([partner, mine], axis=1),
        jnp.concatenate([mine, partner], axis=1),
    )


def shards(
    leaf_coords,
    leaf_modes,
    constraint_modes,
    sep_one,
    sep_two,
    sep_three,
    cluster_rows,
    operators,
    compliance,
    modal_weight,
):
    sub_index = lax.axis_index("sub")
    sub_count = lax.axis_size("sub")
    mode_cols = leaf_coords.shape[1]
    leaf_count = leaf_coords.shape[0]
    leaf_rows = leaf_modes.shape[2]
    dof_count = leaf_count * leaf_rows
    row_ids = cluster_rows.reshape(-1)
    source_dev = row_ids // dof_count
    local_row = row_ids % dof_count
    distance = (source_dev - sub_index) % sub_count
    slot_offset = jnp.where(distance > sub_count // 2, distance - sub_count, distance)
    direct = jnp.einsum("lmk,lkr->mlr", leaf_coords, leaf_modes, preferred_element_type=jnp.float32)
    pieces = [sep_one, sep_two, sep_three]
    for level_bit in range(3):
        active = pieces[level_bit:]
        widths = [piece.shape[1] for piece in active]
        joined = jnp.concatenate(active, axis=1)
        partner = from_partner(joined, "sub", level_bit)
        upper_half = sub_index >> level_bit & 1 == 1
        start = 0
        merged = []
        for width in widths:
            merged.append(
                join_halves(
                    joined[:, start : start + width], partner[:, start : start + width], upper_half
                )
            )
            start = start + width
        pieces = pieces[:level_bit] + merged
    ancestry = jnp.stack(pieces, axis=0)
    coupled = jnp.einsum(
        "amb,labr->mlr", ancestry, constraint_modes, preferred_element_type=jnp.float32
    )
    displaced = (direct + coupled).astype(jnp.bfloat16).reshape(mode_cols, dof_count)
    assembled = jnp.where(
        (slot_offset == 0)[None, :],
        jnp.take(displaced, local_row, axis=1),
        jnp.zeros((), jnp.bfloat16),
    )
    for offset in (-2, -1, 1, 2):
        nearby = passed_along(displaced, "sub", -offset)
        placed = jnp.take(nearby, local_row, axis=1)
        assembled = jnp.where((slot_offset == offset)[None, :], placed, assembled)
    cluster_count = operators.shape[0]
    cluster_width = operators.shape[1]
    blocks = assembled.reshape(mode_cols, cluster_count, cluster_width)
    stresses = jnp.einsum("mck,cks->cms", blocks, operators, preferred_element_type=jnp.float32)
    squared = jnp.sum(stresses * stresses * modal_weight[None, :, None], axis=1) * compliance
    energy_terms = jnp.sum(squared.reshape(cluster_count, 6, -1), axis=1) * (0.5 / M)
    strain_energy = sum_at_owner(energy_terms.reshape(-1), "mode", 0)
    return (stresses, strain_energy)


def solution(mesh):
    return jax.shard_map(
        shards,
        mesh=mesh,
        in_specs=(
            P("sub", "mode", None),
            P("sub", None, None),
            P("sub", None, None, None),
            P("mode", "sub"),
            P("mode", "sub"),
            P("mode", "sub"),
            P("sub", None),
            P("sub", None, None),
            P("sub", None),
            P("mode"),
        ),
        out_specs=(P("sub", "mode", None), P(("sub", "mode"))),
        check_vma=False,
    )
```

profile of v0, /device:TPU:6, one launch (start us, length us, event | category | flops | bytes accessed | tf_op | source)
XLA Modules:
  0.0 137.2 jit_solution(5940276033778759305)
XLA Ops:
  0.6 1.0 copy.32
  1.6 0.8 copy.33
  2.4 0.9 pad_maximum_fusion
  3.4 2.1 %collective-permute-start = (bf16[192,224]{1,0:T(8,128)(2,1)S(1)}, bf16[192,224]{1,0:T(8,128)(2,1)S(1)}, u32[]{:S(2)}, u32[]{:S(2)}) collective-permute-start(bf16[192,224]{1,0:T(8,128)(2,1)S(1)} %pad_maximum_fusion), channel_id=1, source_target_pairs={{0,4},{4,0},{8,12},{12,8},{16,20},{20,16},{24,28},{28,24},{32,36},... | collective-permute-start | bytes 258056 | tf_op jit(solution)/shard_map/ppermute | solution.py:12
  5.4 3.6 %fusion.15 = f32[8,512,192]{1,2,0:T(8,128)} fusion(bf16[8,192,128]{2,1,0:T(8,128)(2,1)} %param.12, bf16[8,128,512]{2,1,0:T(8,128)(2,1)} %param.13), kind=kOutput, calls=%fused_computation.53 | convolution fusion | flops 201326592 | bytes 4587520 | tf_op jit(solution)/shard_map/lmk,lkr->mlr/dot_general | solution.py:62
  9.3 3.5 %collective-permute-start.1 = (bf16[192,192]{1,0:T(8,128)(2,1)S(1)}, bf16[192,192]{1,0:T(8,128)(2,1)S(1)}, u32[]{:S(2)}, u32[]{:S(2)}) collective-permute-start(bf16[192,192]{1,0:T(8,128)(2,1)S(1)} %pad_maximum_fusion.1), channel_id=1, source_target_pairs={{0,8},{4,12},{8,0},{12,4},{16,24},{20,28},{24,16},{28,20},{32,40},... | collective-permute-start | bytes 221192 | tf_op jit(solution)/shard_map/ppermute | solution.py:12
  12.9 3.5 %collective-permute-done.1 = bf16[192,192]{1,0:T(8,128)(2,1)S(1)} collective-permute-done((bf16[192,192]{1,0:T(8,128)(2,1)S(1)}, bf16[192,192]{1,0:T(8,128)(2,1)S(1)}, u32[]{:S(2)}, u32[]{:S(2)}) %collective-permute-start.1) | collective-permute-done | bytes 73760 | tf_op jit(solution)/shard_map/ppermute | solution.py:12
  16.4 0.1 maximum_select_fusion.5
  16.5 4.5 %collective-permute-start.2 = (bf16[192,128]{1,0:T(8,128)(2,1)S(1)}, bf16[192,128]{1,0:T(8,128)(2,1)S(1)}, u32[]{:S(2)}, u32[]{:S(2)}) collective-permute-start(bf16[192,128]{1,0:T(8,128)(2,1)S(1)} %maximum_select_fusion.5), channel_id=1, source_target_pairs={{0,16},{4,20},{8,24},{12,28},{16,0},{20,4},{24,8},{28,12},{32,48},... | collective-permute-start | bytes 147464 | tf_op jit(solution)/shard_map/ppermute | solution.py:12
  21.1 2.6 %collective-permute-done.2 = bf16[192,128]{1,0:T(8,128)(2,1)S(1)} collective-permute-done((bf16[192,128]{1,0:T(8,128)(2,1)S(1)}, bf16[192,128]{1,0:T(8,128)(2,1)S(1)}, u32[]{:S(2)}, u32[]{:S(2)}) %collective-permute-start.2) | collective-permute-done | bytes 49184 | tf_op jit(solution)/shard_map/ppermute | solution.py:12
  23.7 5.1 %fusion.1 = bf16[8,24,8,512]{3,2,1,0:T(8,128)(2,1)S(1)} fusion(bf16[8,3,256,512]{3,2,1,0:T(8,128)(2,1)} %param.14, f32[8,512,192]{1,2,0:T(8,128)} %fusion.15, bf16[1,192,256]{2,1,0:T(8,128)(2,1)S(1)} %maximum_select_fusion.2, bf16[1,192,256]{2,1,0:T(8,128)(2,1)S(1)} %maximum_select_fusion.1, bf16[1,192,256]{2,1,0:T(8,128)(2,1)S(1)} %maximum_select_fusion), kind=kOutput, calls=%fused_computation.7 | convolution fusion | flops 1210417152 | bytes 11304960 | tf_op jit(solution)/shard_map/amb,labr->mlr/dot_general | solution.py:81
  28.8 1.3 copy.47
  30.2 3.2 %collective-permute-start.6 = (bf16[192,4096]{1,0:T(8,128)(2,1)}, bf16[192,4096]{1,0:T(8,128)(2,1)}, u32[]{:S(2)}, u32[]{:S(2)}) collective-permute-start(bf16[192,4096]{1,0:T(8,128)(2,1)} %bitcast.17), channel_id=1, source_target_pairs={{0,8},{4,12},{8,16},{12,20},{16,24},{20,28},{24,32},{28,36},{32,40... | collective-permute-start | bytes 4718600 | tf_op jit(solution)/shard_map/ppermute | solution.py:17
  33.4 1.9 %collective-permute-start.5 = (bf16[192,4096]{1,0:T(8,128)(2,1)}, bf16[192,4096]{1,0:T(8,128)(2,1)}, u32[]{:S(2)}, u32[]{:S(2)}) collective-permute-start(bf16[192,4096]{1,0:T(8,128)(2,1)} %bitcast.17), channel_id=1, source_target_pairs={{0,4},{4,8},{8,12},{12,16},{16,20},{20,24},{24,28},{28,32},{32,36}... | collective-permute-start | bytes 4718600 | tf_op jit(solution)/shard_map/ppermute | solution.py:17
  35.3 6.7 %collective-permute-start.4 = (bf16[192,4096]{1,0:T(8,128)(2,1)}, bf16[192,4096]{1,0:T(8,128)(2,1)}, u32[]{:S(2)}, u32[]{:S(2)}) collective-permute-start(bf16[192,4096]{1,0:T(8,128)(2,1)} %bitcast.17), channel_id=1, source_target_pairs={{0,508},{4,0},{8,4},{12,8},{16,12},{20,16},{24,20},{28,24},{32,28}... | collective-permute-start | bytes 4718600 | tf_op jit(solution)/shard_map/ppermute | solution.py:17
  42.0 2.9 %collective-permute-start.3 = (bf16[192,4096]{1,0:T(8,128)(2,1)}, bf16[192,4096]{1,0:T(8,128)(2,1)}, u32[]{:S(2)}, u32[]{:S(2)}) collective-permute-start(bf16[192,4096]{1,0:T(8,128)(2,1)} %bitcast.17), channel_id=1, source_target_pairs={{0,504},{4,508},{8,0},{12,4},{16,8},{20,12},{24,16},{28,20},{32,24... | collective-permute-start | bytes 4718600 | tf_op jit(solution)/shard_map/ppermute | solution.py:17
  45.0 3.2 %copy.43 = bf16[192,4096]{0,1:T(8,128)(2,1)S(1)} copy(bf16[192,4096]{1,0:T(8,128)(2,1)} %bitcast.17) | data formatting | bytes 3145728 | tf_op jit(solution)/shard_map/reshape | solution.py:84
  48.2 5.4 %gather_fusion.4 = bf16[1536,192]{1,0:T(8,128)(2,1)} fusion(bf16[192,4096]{0,1:T(8,128)(2,1)S(1)} %copy.43, s32[2048]{0:T(1024)S(1)} %pad_clamp_fusion), kind=kCustom, calls=%fused_computation.4.clone | custom fusion | bytes 1185792 | tf_op jit(solution)/shard_map/jit(_take)/gather | solution.py:87
  53.5 19.5 %collective-permute-done.6 = bf16[192,4096]{1,0:T(8,128)(2,1)} collective-permute-done((bf16[192,4096]{1,0:T(8,128)(2,1)}, bf16[192,4096]{1,0:T(8,128)(2,1)}, u32[]{:S(2)}, u32[]{:S(2)}) %collective-permute-start.6) | collective-permute-done | bytes 1572896 | tf_op jit(solution)/shard_map/ppermute | solution.py:17
  73.0 3.1 %copy.42 = bf16[192,4096]{0,1:T(8,128)(2,1)S(1)} copy(bf16[192,4096]{1,0:T(8,128)(2,1)} %collective-permute-done.6) | data formatting | bytes 3145728 | tf_op jit(solution)/shard_map/ppermute | solution.py:17
  76.2 5.4 %gather_fusion.3 = bf16[1536,192]{1,0:T(8,128)(2,1)} fusion(bf16[192,4096]{0,1:T(8,128)(2,1)S(1)} %copy.42, s32[2048]{0:T(1024)S(1)} %pad_clamp_fusion), kind=kCustom, calls=%fused_computation.3.clone | custom fusion | bytes 1185792 | tf_op jit(solution)/shard_map/jit(_take)/gather | solution.py:92
  81.5 6.1 %collective-permute-done.5 = bf16[192,4096]{1,0:T(8,128)(2,1)} collective-permute-done((bf16[192,4096]{1,0:T(8,128)(2,1)}, bf16[192,4096]{1,0:T(8,128)(2,1)}, u32[]{:S(2)}, u32[]{:S(2)}) %collective-permute-start.5) | collective-permute-done | bytes 1572896 | tf_op jit(solution)/shard_map/ppermute | solution.py:17
  87.6 3.1 %copy.41 = bf16[192,4096]{0,1:T(8,128)(2,1)S(1)} copy(bf16[192,4096]{1,0:T(8,128)(2,1)} %collective-permute-done.5) | data formatting | bytes 3145728 | tf_op jit(solution)/shard_map/ppermute | solution.py:17
  90.8 5.4 %gather_fusion.2 = bf16[1536,192]{1,0:T(8,128)(2,1)} fusion(bf16[192,4096]{0,1:T(8,128)(2,1)S(1)} %copy.41, s32[2048]{0:T(1024)S(1)} %pad_clamp_fusion), kind=kCustom, calls=%fused_computation.2.clone | custom fusion | bytes 1185792 | tf_op jit(solution)/shard_map/jit(_take)/gather | solution.py:92
  96.2 3.1 %copy.40 = bf16[192,4096]{0,1:T(8,128)(2,1)S(1)} copy(bf16[192,4096]{1,0:T(8,128)(2,1)} %collective-permute-done.4) | data formatting | bytes 3145728 | tf_op jit(solution)/shard_map/ppermute | solution.py:17
  99.3 5.4 %gather_fusion.1 = bf16[1536,192]{1,0:T(8,128)(2,1)} fusion(bf16[192,4096]{0,1:T(8,128)(2,1)S(1)} %copy.40, s32[2048]{0:T(1024)S(1)} %pad_clamp_fusion), kind=kCustom, calls=%fused_computation.1.clone | custom fusion | bytes 1185792 | tf_op jit(solution)/shard_map/jit(_take)/gather | solution.py:92
  104.7 3.1 %copy.39 = bf16[192,4096]{0,1:T(8,128)(2,1)S(1)} copy(bf16[192,4096]{1,0:T(8,128)(2,1)} %collective-permute-done.3) | data formatting | bytes 3145728 | tf_op jit(solution)/shard_map/ppermute | solution.py:17
  107.8 5.4 %gather_fusion = bf16[1536,192]{1,0:T(8,128)(2,1)} fusion(bf16[192,4096]{0,1:T(8,128)(2,1)S(1)} %copy.39, s32[2048]{0:T(1024)S(1)} %pad_clamp_fusion), kind=kCustom, calls=%fused_computation.clone | custom fusion | bytes 1185792 | tf_op jit(solution)/shard_map/jit(_take)/gather | solution.py:92
  113.2 4.8 %fusion.5 = bf16[192,1536]{0,1:T(8,128)(2,1)S(1)} fusion(bf16[1536,192]{1,0:T(8,128)(2,1)} %gather_fusion.4, bf16[1536,192]{1,0:T(8,128)(2,1)} %gather_fusion.3, bf16[1536,192]{1,0:T(8,128)(2,1)} %gather_fusion.2, bf16[1536,192]{1,0:T(8,128)(2,1)} %gather_fusion.1, bf16[1536,192]{1,0:T(8,128)(2,1)} %gather_fusion, pred[1536]{0:T(1024)(128)(4,1)S(1)} %get-tuple-element.11, ...), kind=kLoop, calls=%fused_computation.13 | loop fusion | flops 2949120 | bytes 3548160 | tf_op jit(solution)/shard_map/jit(_where)/select_n | solution.py:93
  118.0 1.4 %multiply_reduce_fusion = (f32[3,384]{1,0:T(4,128)S(1)}, f32[3,192,384]{2,1,0:T(8,128)}) fusion(f32[192]{0:T(256)S(1)} %copy-done.4, bf16[192,3,512]{0,2,1:T(8,128)(2,1)S(1)} %bitcast.49, bf16[3,512,384]{2,1,0:T(8,128)(2,1)S(1)} %copy-done), kind=kOutput, calls=%fused_computation.8 | convolution fusion | flops 227154816 | bytes 2659584 | tf_op jit(solution)/shard_map/mck,cks->cms/dot_general | solution.py:97
  119.7 17.0 %all_to_all.6 = f32[4,1,48]{2,1,0:T(1,128)S(1)} all-to-all(f32[4,1,48]{2,1,0:T(1,128)S(1)} %mul.37), channel_id=1, replica_groups=mesh['sub'=128,'mode'=4] {'mode'}, dimensions={0} | all-to-all | bytes 1536 | tf_op jit(solution)/shard_map/all_to_all | solution.py:27
  136.7 0.5 reduce_sum.29
  (33 shorter events, 0.7 us)
Async XLA Ops:
  0.6 117.4 %copy-start = (bf16[3,512,384]{2,1,0:T(8,128)(2,1)S(1)}, bf16[3,512,384]{2,1,0:T(8,128)(2,1)}, u32[]{:S(2)}) copy-start(bf16[3,512,384]{2,1,0:T(8,128)(2,1)} %param.19) | copy-start | bytes 3538948
  3.3 9.5 %copy-start.1 = (bf16[192,128]{1,0:T(8,128)(2,1)S(1)}, bf16[192,128]{1,0:T(8,128)(2,1)}, u32[]{:S(2)}) copy-start(bf16[192,128]{1,0:T(8,128)(2,1)} %param.15) | copy-start | bytes 147460
  3.4 5.6 %collective-permute-start = (bf16[192,224]{1,0:T(8,128)(2,1)S(1)}, bf16[192,224]{1,0:T(8,128)(2,1)S(1)}, u32[]{:S(2)}, u32[]{:S(2)}) collective-permute-start(bf16[192,224]{1,0:T(8,128)(2,1)S(1)} %pad_maximum_fusion), channel_id=1, source_target_pairs={{0,4},{4,0},{8,12},{12,8},{16,20},{20,16},{24,28},{28,24},{32,36},... | collective-permute-start | bytes 258056 | tf_op jit(solution)/shard_map/ppermute | solution.py:12
  9.3 7.1 %collective-permute-start.1 = (bf16[192,192]{1,0:T(8,128)(2,1)S(1)}, bf16[192,192]{1,0:T(8,128)(2,1)S(1)}, u32[]{:S(2)}, u32[]{:S(2)}) collective-permute-start(bf16[192,192]{1,0:T(8,128)(2,1)S(1)} %pad_maximum_fusion.1), channel_id=1, source_target_pairs={{0,8},{4,12},{8,0},{12,4},{16,24},{20,28},{24,16},{28,20},{32,40},... | collective-permute-start | bytes 221192 | tf_op jit(solution)/shard_map/ppermute | solution.py:12
  16.5 7.2 %collective-permute-start.2 = (bf16[192,128]{1,0:T(8,128)(2,1)S(1)}, bf16[192,128]{1,0:T(8,128)(2,1)S(1)}, u32[]{:S(2)}, u32[]{:S(2)}) collective-permute-start(bf16[192,128]{1,0:T(8,128)(2,1)S(1)} %maximum_select_fusion.5), channel_id=1, source_target_pairs={{0,16},{4,20},{8,24},{12,28},{16,0},{20,4},{24,8},{28,12},{32,48},... | collective-permute-start | bytes 147464 | tf_op jit(solution)/shard_map/ppermute | solution.py:12
  28.8 16.1 %copy-start.2 = (s32[3,512]{1,0:T(4,128)S(1)}, s32[3,512]{1,0:T(4,128)}, u32[]{:S(2)}) copy-start(s32[3,512]{1,0:T(4,128)} %param.18) | copy-start | bytes 18436
  30.2 42.8 %collective-permute-start.6 = (bf16[192,4096]{1,0:T(8,128)(2,1)}, bf16[192,4096]{1,0:T(8,128)(2,1)}, u32[]{:S(2)}, u32[]{:S(2)}) collective-permute-start(bf16[192,4096]{1,0:T(8,128)(2,1)} %bitcast.17), channel_id=1, source_target_pairs={{0,8},{4,12},{8,16},{12,20},{16,24},{20,28},{24,32},{28,36},{32,40... | collective-permute-start | bytes 4718600 | tf_op jit(solution)/shard_map/ppermute | solution.py:17
  33.4 54.3 %collective-permute-start.5 = (bf16[192,4096]{1,0:T(8,128)(2,1)}, bf16[192,4096]{1,0:T(8,128)(2,1)}, u32[]{:S(2)}, u32[]{:S(2)}) collective-permute-start(bf16[192,4096]{1,0:T(8,128)(2,1)} %bitcast.17), channel_id=1, source_target_pairs={{0,4},{4,8},{8,12},{12,16},{16,20},{20,24},{24,28},{28,32},{32,36}... | collective-permute-start | bytes 4718600 | tf_op jit(solution)/shard_map/ppermute | solution.py:17
  35.3 60.9 %collective-permute-start.4 = (bf16[192,4096]{1,0:T(8,128)(2,1)}, bf16[192,4096]{1,0:T(8,128)(2,1)}, u32[]{:S(2)}, u32[]{:S(2)}) collective-permute-start(bf16[192,4096]{1,0:T(8,128)(2,1)} %bitcast.17), channel_id=1, source_target_pairs={{0,508},{4,0},{8,4},{12,8},{16,12},{20,16},{24,20},{28,24},{32,28}... | collective-permute-start | bytes 4718600 | tf_op jit(solution)/shard_map/ppermute | solution.py:17
  42.0 62.7 %collective-permute-start.3 = (bf16[192,4096]{1,0:T(8,128)(2,1)}, bf16[192,4096]{1,0:T(8,128)(2,1)}, u32[]{:S(2)}, u32[]{:S(2)}) collective-permute-start(bf16[192,4096]{1,0:T(8,128)(2,1)} %bitcast.17), channel_id=1, source_target_pairs={{0,504},{4,508},{8,0},{12,4},{16,8},{20,12},{24,16},{28,20},{32,24... | collective-permute-start | bytes 4718600 | tf_op jit(solution)/shard_map/ppermute | solution.py:17
  113.2 4.8 %copy-start.4 = (f32[192]{0:T(256)S(1)}, f32[192]{0:T(256)}, u32[]{:S(2)}) copy-start(f32[192]{0:T(256)} %param.21) | copy-start | bytes 2308
  118.0 1.5 %copy-start.3 = (f32[3,384]{1,0:T(4,128)S(1)}, f32[3,384]{1,0:T(4,128)}, u32[]{:S(2)}) copy-start(f32[3,384]{1,0:T(4,128)} %param.20) | copy-start | bytes 13828
where the time goes:
time: 138 us; the launch traced here: 137 us
  local copies, waits for them, and re-layouts  46 us (33%)
  waiting for transfers between devices  31.7 us (23%)
  starting transfers between devices  24.7 us (18%)
  blocking collectives  17 us (12%)
  matrix products  10.1 us (7%)
  other arithmetic  6.7 us (5%)
    ppermute x4, waiting for transfers between devices, passed_along(): lax.ppermute(shard, axis, [(i, (i + by) % peers) for i in range(peers)])  25.6 us
    gather x4, local copies, waits for them, and re-layouts, shards(): placed = jnp.take(nearby, local_row, axis=1)  21.4 us
    all_to_all x1, blocking collectives, sum_at_owner(): parts = lax.all_to_all(in_blocks(shard, dim, peers), axis, 0, 0, tiled=True)  17 us
    ppermute x4, starting transfers between devices, passed_along(): lax.ppermute(shard, axis, [(i, (i + by) % peers) for i in range(peers)])  14.7 us
    ppermute x4, local copies, waits for them, and re-layouts, passed_along(): lax.ppermute(shard, axis, [(i, (i + by) % peers) for i in range(peers)])  12.6 us
    ppermute x3, starting transfers between devices, from_partner(): return lax.ppermute(value, axis, pairs)  10 us
    ppermute x3, waiting for transfers between devices, from_partner(): return lax.ppermute(value, axis, pairs)  6.15 us
    gather x1, local copies, waits for them, and re-layouts, shards(): jnp.take(displaced, local_row, axis=1)  5.36 us
  transfers between devices with their start and end apart: 7, of which 4 were waited for; matrix products, arithmetic and copies ran while one was open for 27% of the time, Pallas kernels for 0%

commit v1 on v0

v1 whole, which is shorter than its diff:
```python
import functools

import jax
import jax.numpy as jnp
from jax import lax
from jax.experimental import pallas as pl
from jax.experimental.pallas import tpu as pltpu
from jax.sharding import PartitionSpec as P

M = 768
F32, BF16 = jnp.float32, jnp.bfloat16
MODES, NLEAF, KL, R, B = 192, 8, 128, 512, 256
DOFS = NLEAF * R
CLS, CW, SR = 3, 512, 384
SLOT, NOFF = 384, 5
MESH = pl.DeviceIdType.MESH


def mm(a, b):
    return jnp.dot(a, b, preferred_element_type=F32)


def one_hot(table, values):
    n, w = table.shape[0], values.shape[1]
    wide = jnp.broadcast_to(values, (16, w)).astype(BF16).reshape(1, 16, w)
    rows = jnp.concatenate([table.reshape(n // 16, 16, 128)] * (w // 128), axis=2)
    hit = rows == jnp.broadcast_to(wide, (n // 16, 16, w))
    return jnp.where(hit, jnp.ones((), BF16), jnp.zeros((), BF16)).reshape(n, w)


def kernel(
    subs,
    peers_mode,
    lc_h,
    lm_h,
    cm_h,
    s1_h,
    s2_h,
    s3_h,
    rows_h,
    ops_h,
    comp_h,
    mw_h,
    stress,
    energy,
    lc,
    w,
    a1,
    a2,
    a3,
    x23,
    rows,
    ops,
    comp,
    mw,
    acc,
    disp,
    table,
    pick,
    perm,
    lists,
    want,
    hot,
    gath,
    got,
    sacc,
    terms,
    in_sem,
    leaf_sem,
    cm_sem,
    sep_send,
    sep_recv,
    list_send,
    list_recv,
    data_send,
    data_recv,
    en_send,
    en_recv,
):
    me = lax.axis_index("sub")
    mo = lax.axis_index("mode")
    odd = lax.rem(me, 2)
    in_eight = lax.rem(me, 8)
    in_four = lax.rem(me, 4)
    rows[...] = jnp.full(rows.shape, -1, jnp.int32)

    own1 = a1.at[:, pl.ds(pl.multiple_of(odd * 128, 128), 128)]
    own2 = a2.at[pl.ds(pl.multiple_of(in_four * 64, 64), 64), :]
    own3 = a3.at[pl.ds(pl.multiple_of(in_eight * 32, 32), 32), :]
    loads = [
        pltpu.make_async_copy(s3_h, own3, in_sem.at[0]),
        pltpu.make_async_copy(s2_h, own2, in_sem.at[1]),
        pltpu.make_async_copy(s1_h, own1, in_sem.at[2]),
        pltpu.make_async_copy(rows_h, rows.at[pl.ds(0, CLS), :], in_sem.at[3]),
        pltpu.make_async_copy(lc_h, lc, in_sem.at[4]),
        pltpu.make_async_copy(comp_h, comp, in_sem.at[5]),
        pltpu.make_async_copy(mw_h, mw, in_sem.at[6]),
        pltpu.make_async_copy(ops_h, ops, in_sem.at[7]),
    ]
    for load in loads[:7]:
        load.start()

    def leaf_load(l):
        return pltpu.make_async_copy(lm_h.at[l], w.at[l, pl.ds(0, KL), :], leaf_sem.at[l])

    def cm_load(l):
        return pltpu.make_async_copy(cm_h.at[l], w.at[l, pl.ds(KL, 3 * B), :], cm_sem.at[l])

    @pl.loop(0, NLEAF)
    def _(l):
        leaf_load(l).start()
        cm_load(l).start()

    loads[7].start()

    def at_sub(offset):
        return lax.rem(me + offset + subs, subs)

    def in_group(x):
        return me - in_eight + jnp.bitwise_xor(in_eight, x)

    barrier = pltpu.get_barrier_semaphore()
    greeted = 0
    for x in range(1, 8):
        pl.semaphore_signal(barrier, inc=1, device_id=(in_group(x), mo), device_id_type=MESH)
        greeted += 1
    for q in (-2, -1, 1, 2):
        pl.semaphore_signal(barrier, inc=1, device_id=(at_sub(q), mo), device_id_type=MESH)
        greeted += 1
    for x in range(1, peers_mode):
        other = lax.rem(mo + x, peers_mode)
        pl.semaphore_signal(barrier, inc=1, device_id=(me, other), device_id_type=MESH)
        greeted += 1

    table[...] = (lax.broadcasted_iota(jnp.int32, (R, 128), 0) - 256).astype(F32).astype(BF16)
    loads[3].wait()
    ids = rows[...]
    off = jnp.bitwise_and(jnp.right_shift(ids, 12) - me + 2, subs - 1)
    off = jnp.where(ids < 0, -1, off)
    local = jnp.bitwise_and(ids, DOFS - 1)
    masks = jnp.concatenate([(off == o).astype(F32) for o in range(NOFF + 1)], axis=0)
    earlier = (
        lax.broadcasted_iota(jnp.int32, (CW, CW), 0) < lax.broadcasted_iota(jnp.int32, (CW, CW), 1)
    )
    ranks = mm(masks.astype(BF16), jnp.where(earlier, 1.0, 0.0).astype(BF16))
    totals = jnp.sum(masks, axis=1, keepdims=True)
    place = lax.broadcasted_iota(jnp.int32, (8, 1), 0)
    wanted = []
    for o in range(NOFF):
        count = totals[8 * o : 8 * o + 8]
        base = jnp.where(place >= 1, count[0:1], 0.0) + jnp.where(place >= 2, count[1:2], 0.0)
        rank = ranks[8 * o : 8 * o + 8] + base
        wanted.append(jnp.where(off == o, rank - SLOT // 2, 999.0))

    pl.semaphore_wait(barrier, greeted)

    for load in loads[:3]:
        load.wait()
    sends = []
    for n, x in enumerate((7, 6, 5, 4, 3, 2, 1)):
        sends.append((own3, own3, n, x))
    for n, x in enumerate((3, 2, 1)):
        sends.append((own2, own2, 7 + n, x))
    sends.append((own1, own1, 10, 1))
    sep_copies = [
        pltpu.make_async_remote_copy(
            src_ref=src,
            dst_ref=dst,
            send_sem=sep_send.at[n],
            recv_sem=sep_recv.at[n],
            device_id=(in_group(x), mo),
            device_id_type=MESH,
        )
        for src, dst, n, x in sends
    ]
    for copy in sep_copies:
        copy.start()

    values = jnp.concatenate(
        [
            jnp.right_shift(local, 6).astype(F32),
            jnp.bitwise_and(local, 63).astype(F32),
        ],
        axis=0,
    ).astype(BF16)
    for o in range(NOFF):
        parts = None
        for c in range(CLS):
            hit = one_hot(table[256 - SLOT // 2 : 256 + SLOT // 2], wanted[o][c : c + 1])
            pick[o, :, c * CW : (c + 1) * CW] = hit
            part = lax.dot_general(values, hit, (((1,), (1,)), ((), ())), preferred_element_type=F32)
            part = part[c : c + 1] * 64.0 + part[8 + c : 9 + c]
            parts = part if parts is None else parts + part
        lists[o] = parts.astype(jnp.int32)

    def list_copy(o, target):
        return pltpu.make_async_remote_copy(
            src_ref=lists.at[o],
            dst_ref=want.at[o],
            send_sem=list_send.at[o],
            recv_sem=list_recv.at[o],
            device_id=(target, mo),
            device_id_type=MESH,
        )

    far = (0, 1, 3, 4)
    list_copies = {o: list_copy(o, at_sub(o - 2)) for o in far}
    for o in far:
        list_copies[o].start()

    loads[4].wait()
    sep_copies[10].wait_recv()

    @pl.loop(0, NLEAF)
    def _(l):
        leaf_load(l).wait()
        cm_load(l).wait()
        x = jnp.concatenate([lc[l], a1[...]], axis=1)
        acc[l] = mm(x, w[l, 0 : KL + B, :])

    for n in range(7, 10):
        sep_copies[n].wait_recv()
    x23[:, 0:B] = jnp.transpose(a2[...])
    for n in range(7):
        sep_copies[n].wait_recv()
    x23[:, B : 2 * B] = jnp.transpose(a3[...])

    @pl.loop(0, NLEAF)
    def _(l):
        both = acc[l] + mm(x23[...], w[l, KL + B : KL + 3 * B, :])
        disp[:, pl.ds(pl.multiple_of(l * R, R), R)] = both.astype(BF16)

    def gather(o, wish, into):
        for l in range(NLEAF):
            here = jnp.right_shift(wish, 9) == l
            v = jnp.where(here, jnp.bitwise_and(wish, R - 1) - 256, 999).astype(F32)
            hot[l * R : (l + 1) * R, :] = one_hot(table[...], v)
        into[o] = mm(disp[...], hot[...]).astype(BF16)

    third = 3 - 2 * odd
    order = (0, 4, third, 4 - third)
    data_copies = []
    for o in order:
        list_copy(o, me).wait_recv()
        gather(o, want[o], gath)
        copy = pltpu.make_async_remote_copy(
            src_ref=gath.at[o],
            dst_ref=got.at[o],
            send_sem=data_send.at[o],
            recv_sem=data_recv.at[o],
            device_id=(at_sub(2 - o), mo),
            device_id_type=MESH,
        )
        copy.start()
        data_copies.append(copy)
    gather(2, lists[2], got)

    loads[7].wait()

    @pl.loop(0, NOFF)
    def _(o):
        for c in range(CLS):
            moved = mm(pick[o, :, c * CW : (c + 1) * CW], ops[c])
            perm[o, :, c * SR : (c + 1) * SR] = moved.astype(BF16)

    loads[5].wait()
    loads[6].wait()
    eye = lax.broadcasted_iota(jnp.int32, (MODES, MODES), 0) == lax.broadcasted_iota(
        jnp.int32, (MODES, MODES), 1
    )
    weight = jnp.sum(jnp.where(eye, mw[...], 0.0), axis=1, keepdims=True)

    def arrived(o):
        pltpu.make_async_remote_copy(
            src_ref=gath.at[o],
            dst_ref=got.at[o],
            send_sem=data_send.at[o],
            recv_sem=data_recv.at[o],
            device_id=(me, mo),
            device_id_type=MESH,
        ).wait_recv()

    sacc[...] = mm(got[2], perm[2])
    last = 4 - third
    for o in (0, 4, third):
        arrived(o)
        sacc[...] += mm(got[o], perm[o])
    arrived(last)
    energies = []
    for c in range(CLS):
        cols = slice(c * SR, (c + 1) * SR)
        s = sacc[:, cols] + mm(got[last], perm[last, :, cols])
        stress[c] = s
        e = jnp.sum(s * s * weight, axis=0, keepdims=True) * comp[c : c + 1]
        e = e[:, 0:128] + e[:, 128:256] + e[:, 256:384]
        energies.append((e + pltpu.roll(e, 64, 1)) * (0.5 / M))
    low = lax.broadcasted_iota(jnp.int32, (1, 128), 1) < 64
    mine = jnp.concatenate([jnp.where(low, energies[0], energies[1]), energies[2]], axis=1)
    terms[mo] = mine
    en_copies = []
    for x in range(1, peers_mode):
        other = lax.rem(mo + x, peers_mode)
        copy = pltpu.make_async_remote_copy(
            src_ref=terms.at[mo],
            dst_ref=terms.at[mo],
            send_sem=en_send.at[x],
            recv_sem=en_recv.at[x],
            device_id=(me, other),
            device_id_type=MESH,
        )
        copy.start()
        en_copies.append(copy)
    for copy in en_copies:
        copy.wait_recv()
    total = terms[0]
    for x in range(1, peers_mode):
        total = total + terms[x]
    share = CLS * 64 // peers_mode
    total = pltpu.roll(total, lax.rem(256 - share * mo, 256), 1)
    energy[...] = total[:, 0:share]

    for copy in sep_copies:
        copy.wait_send()
    for o in far:
        list_copies[o].wait_send()
    for copy in data_copies:
        copy.wait_send()
    for copy in en_copies:
        copy.wait_send()


def shards(lc, lm, cm, s1, s2, s3, rows, ops, comp, mw):
    subs = lax.axis_size("sub")
    peers_mode = lax.axis_size("mode")
    share = CLS * 64 // peers_mode
    anywhere = pl.BlockSpec(memory_space=pl.ANY)
    vmem = pl.BlockSpec(memory_space=pltpu.VMEM)
    dma = pltpu.SemaphoreType.DMA
    stress, energy = pl.pallas_call(
        functools.partial(kernel, subs, peers_mode),
        out_shape=(
            jax.ShapeDtypeStruct((CLS, MODES, SR), F32),
            jax.ShapeDtypeStruct((1, share), F32),
        ),
        in_specs=[anywhere] * 10,
        out_specs=(vmem, vmem),
        scratch_shapes=[
            pltpu.VMEM((NLEAF, MODES, KL), BF16),
            pltpu.VMEM((NLEAF, KL + 3 * B, R), BF16),
            pltpu.VMEM((MODES, B), BF16),
            pltpu.VMEM((B, MODES), BF16),
            pltpu.VMEM((B, MODES), BF16),
            pltpu.VMEM((MODES, 2 * B), BF16),
            pltpu.VMEM((8, CW), jnp.int32),
            pltpu.VMEM((CLS, CW, SR), BF16),
            pltpu.VMEM((CLS, SR), F32),
            pltpu.VMEM((1, MODES), F32),
            pltpu.VMEM((NLEAF, MODES, R), F32),
            pltpu.VMEM((MODES, DOFS), BF16),
            pltpu.VMEM((R, 128), BF16),
            pltpu.VMEM((NOFF, SLOT, CLS * CW), BF16),
            pltpu.VMEM((NOFF, SLOT, CLS * SR), BF16),
            pltpu.VMEM((NOFF, 1, SLOT), jnp.int32),
            pltpu.VMEM((NOFF, 1, SLOT), jnp.int32),
            pltpu.VMEM((DOFS, SLOT), BF16),
            pltpu.VMEM((NOFF, MODES, SLOT), BF16),
            pltpu.VMEM((NOFF, MODES, SLOT), BF16),
            pltpu.VMEM((MODES, CLS * SR), F32),
            pltpu.VMEM((peers_mode, 1, 256), F32),
            dma((8,)),
            dma((NLEAF,)),
            dma((NLEAF,)),
            dma((11,)),
            dma((11,)),
            dma((NOFF,)),
            dma((NOFF,)),
            dma((NOFF,)),
            dma((NOFF,)),
            dma((4,)),
            dma((4,)),
        ],
        compiler_params=pltpu.CompilerParams(
            collective_id=0, has_side_effects=True, vmem_limit_bytes=56 * 2**20
        ),
        name="back_transform",
    )(
        lc,
        lm,
        cm.reshape(NLEAF, 3 * B, R),
        s1,
        s2.T,
        s3.T,
        rows,
        ops,
        comp,
        mw.reshape(1, MODES),
    )
    return stress, energy.reshape(share)


def solution(mesh):
    return jax.shard_map(
        shards,
        mesh=mesh,
        in_specs=(
            P("sub", "mode", None),
            P("sub", None, None),
            P("sub", None, None, None),
            P("mode", "sub"),
            P("mode", "sub"),
            P("mode", "sub"),
            P("sub", None),
            P("sub", None, None),
            P("sub", None),
            P("mode"),
        ),
        out_specs=(P("sub", "mode", None), P(("sub", "mode"))),
        check_vma=False,
    )
```

time: 138 us -> 41.7 us (0.30)
  the two profiles are of different devices: /device:TPU:6 before, /device:TPU:8 now
where the time goes in v1:
time: 41.7 us; the launch traced here: 41.6 us
  Pallas kernels  37.6 us (90%)
  local copies, waits for them, and re-layouts  3.31 us (8%)
  between operations  0.64 us (2%)
    pallas_call x1, Pallas kernels, shards(): pl.pallas_call(functools.partial(kernel, subs, peers_mode), out_shape=(ja...  37.6 us
    unnamed x2, local copies, waits for them, and re-layouts  3.31 us

profile of v1, /device:TPU:8, one launch (start us, length us, event | category | flops | bytes accessed | tf_op | source)
XLA Modules:
  0.0 41.6 jit_solution(1200325639362581813)
XLA Ops:
  0.6 37.6 %back_transform.1 = (f32[3,192,384]{2,1,0:T(8,128)}, f32[1,48]{1,0:T(1,128)}) custom-call(bf16[8,192,128]{2,1,0:T(8,128)(2,1)} %lc_h.1, bf16[8,128,512]{2,1,0:T(8,128)(2,1)} %lm_h.1, bf16[8,768,512]{2,1,0:T(8,128)(2,1)} %bitcast.5, bf16[192,128]{1,0:T(8,128)(2,1)} %s1_h.1, bf16[64,192]{1,0:T(8,128)(2,1)} %bitcast.6, bf16[32,192]{1,0:T(8,128)(2,1)} %bitcast.7, ...), custom_call_target="tpu_custom_call" | custom-call | tf_op jit(solution)/shard_map/back_transform/pallas_call | solution.py:339
  38.3 2.1 %copy.14 = f32[3,192,384]{2,1,0:T(8,128)} copy(f32[3,192,384]{2,1,0:T(8,128)} %get-tuple-element.8) | data formatting | bytes 1769472
  40.4 1.2 %copy.15 = f32[48]{0:T(128)} copy(f32[48]{0:T(128)} %bitcast.9) | data formatting | bytes 384

commit v2 on v1

v2 whole, which is shorter than its diff:
```python
import functools

import jax
import jax.numpy as jnp
from jax import lax
from jax.experimental import pallas as pl
from jax.experimental.pallas import tpu as pltpu
from jax.sharding import PartitionSpec as P

M = 768
F32, BF16 = jnp.float32, jnp.bfloat16
MODES, NLEAF, KL, R, B = 192, 8, 128, 512, 256
DOFS = NLEAF * R
CLS, CW, SR = 3, 512, 384
SLOT, NOFF = 384, 5
MESH = pl.DeviceIdType.MESH


def mm(a, b):
    return jnp.dot(a, b, preferred_element_type=F32)


def one_hot(table, values):
    n, w = table.shape[0], values.shape[1]
    wide = jnp.broadcast_to(values, (16, w)).astype(BF16).reshape(1, 16, w)
    rows = jnp.concatenate([table.reshape(n // 16, 16, 128)] * (w // 128), axis=2)
    hit = rows == jnp.broadcast_to(wide, (n // 16, 16, w))
    return jnp.where(hit, jnp.ones((), BF16), jnp.zeros((), BF16)).reshape(n, w)


def kernel(
    subs,
    peers_mode,
    lc_h,
    lm_h,
    cm_h,
    s1_h,
    s2_h,
    s3_h,
    rows_h,
    ops_h,
    comp_h,
    mw_h,
    cols_h,
    energy,
    lc,
    w,
    a1,
    a2,
    a3,
    x23,
    rows,
    ops,
    comp,
    mw,
    acc,
    disp,
    table,
    pick,
    lists,
    want,
    hot,
    own_hot,
    gath,
    got,
    cols32,
    cols,
    terms,
    in_sem,
    leaf_sem,
    cm_sem,
    sep_send,
    sep_recv,
    list_send,
    list_recv,
    data_send,
    data_recv,
    en_send,
    en_recv,
):
    me = lax.axis_index("sub")
    mo = lax.axis_index("mode")
    odd = lax.rem(me, 2)
    in_eight = lax.rem(me, 8)
    in_four = lax.rem(me, 4)

    def at_sub(offset):
        return lax.rem(me + offset + subs, subs)

    def in_group(x):
        return me - in_eight + jnp.bitwise_xor(in_eight, x)

    barrier = pltpu.get_barrier_semaphore()
    greeted = 0
    for x in range(1, 8):
        pl.semaphore_signal(barrier, inc=1, device_id=(in_group(x), mo), device_id_type=MESH)
        greeted += 1
    for q in (-2, -1, 1, 2):
        pl.semaphore_signal(barrier, inc=1, device_id=(at_sub(q), mo), device_id_type=MESH)
        greeted += 1
    for x in range(1, peers_mode):
        other = lax.rem(mo + x, peers_mode)
        pl.semaphore_signal(barrier, inc=1, device_id=(me, other), device_id_type=MESH)
        greeted += 1

    rows[...] = jnp.full(rows.shape, -1, jnp.int32)
    own1 = a1.at[:, pl.ds(pl.multiple_of(odd * 128, 128), 128)]
    own2 = a2.at[pl.ds(pl.multiple_of(in_four * 64, 64), 64), :]
    own3 = a3.at[pl.ds(pl.multiple_of(in_eight * 32, 32), 32), :]
    loads = [
        pltpu.make_async_copy(rows_h, rows.at[pl.ds(0, CLS), :], in_sem.at[0]),
        pltpu.make_async_copy(s3_h, own3, in_sem.at[1]),
        pltpu.make_async_copy(s2_h, own2, in_sem.at[2]),
        pltpu.make_async_copy(s1_h, own1, in_sem.at[3]),
        pltpu.make_async_copy(lc_h, lc, in_sem.at[4]),
        pltpu.make_async_copy(comp_h, comp, in_sem.at[5]),
        pltpu.make_async_copy(mw_h, mw, in_sem.at[6]),
        pltpu.make_async_copy(ops_h, ops, in_sem.at[7]),
    ]
    for load in loads[:4]:
        load.start()
    pl.semaphore_wait(barrier, greeted)

    sends = [(s3_h, own3, n, x) for n, x in enumerate((7, 6, 5, 4, 3, 2, 1))]
    sends += [(s2_h, own2, 7 + n, x) for n, x in enumerate((3, 2, 1))]
    sends.append((s1_h, own1, 10, 1))
    sep_copies = [
        pltpu.make_async_remote_copy(
            src_ref=src,
            dst_ref=dst,
            send_sem=sep_send.at[n],
            recv_sem=sep_recv.at[n],
            device_id=(in_group(x), mo),
            device_id_type=MESH,
        )
        for src, dst, n, x in sends
    ]
    for copy in sep_copies:
        copy.start()

    def leaf_load(l):
        return pltpu.make_async_copy(lm_h.at[l], w.at[l, pl.ds(0, KL), :], leaf_sem.at[l])

    def cm_load(l):
        return pltpu.make_async_copy(cm_h.at[l], w.at[l, pl.ds(KL, 3 * B), :], cm_sem.at[l])

    loads[4].start()
    for l in range(NLEAF):
        leaf_load(l).start()
        cm_load(l).start()
    for load in loads[5:]:
        load.start()

    table[...] = (lax.broadcasted_iota(jnp.int32, (R, 128), 0) - 256).astype(F32).astype(BF16)
    earlier = (
        lax.broadcasted_iota(jnp.int32, (CW, CW), 0) < lax.broadcasted_iota(jnp.int32, (CW, CW), 1)
    )
    earlier = jnp.where(earlier, 1.0, 0.0).astype(BF16)
    loads[0].wait()
    ids = rows[...]
    off = jnp.bitwise_and(jnp.right_shift(ids, 12) - me + 2, subs - 1)
    off = jnp.where(ids < 0, -1, off)
    local = jnp.bitwise_and(ids, DOFS - 1)
    masks = jnp.concatenate([(off == o).astype(F32) for o in range(NOFF + 1)], axis=0)
    ranks = mm(masks.astype(BF16), earlier)
    totals = jnp.sum(masks, axis=1, keepdims=True)
    line = lax.broadcasted_iota(jnp.int32, (8, 1), 0)
    wanted = []
    slot = jnp.full((8, CW), -1, jnp.int32)
    for o in range(NOFF):
        count = totals[8 * o : 8 * o + 8]
        base = jnp.where(line >= 1, count[0:1], 0.0) + jnp.where(line >= 2, count[1:2], 0.0)
        rank = ranks[8 * o : 8 * o + 8] + base
        wanted.append(jnp.where(off == o, rank - SLOT // 2, 999.0))
        slot = jnp.where(off == o, rank.astype(jnp.int32) + SLOT * o, slot)
    slot_row, slot_col = jnp.right_shift(slot, 7), jnp.bitwise_and(slot, 127)
    high, low = jnp.right_shift(local, 6), jnp.bitwise_and(local, 63)
    sixteen = lax.broadcasted_iota(jnp.int32, (16, CW), 0)
    left, right = [], []
    for c in range(CLS):
        here = slot_row[c : c + 1] == sixteen
        both = [jnp.where(here, part[c : c + 1], 0) for part in (high, low)]
        left.append(jnp.concatenate(both, axis=0).astype(F32).astype(BF16))
        right.append(one_hot(table[256:384], slot_col[c : c + 1].astype(F32)))
    found = lax.dot_general(
        jnp.concatenate(left, axis=1),
        jnp.concatenate(right, axis=1),
        (((1,), (1,)), ((), ())),
        preferred_element_type=F32,
    )
    found = (found[0:16] * 64.0 + found[16:32]).astype(jnp.int32)
    for r in range(3 * NOFF):
        lists[r] = found[r : r + 1]

    def list_copy(o, target):
        return pltpu.make_async_remote_copy(
            src_ref=lists.at[pl.ds(3 * o, 3)],
            dst_ref=want.at[pl.ds(3 * o, 3)],
            send_sem=list_send.at[o],
            recv_sem=list_recv.at[o],
            device_id=(target, mo),
            device_id_type=MESH,
        )

    far = (0, 4, 1, 3)
    list_copies = [list_copy(o, at_sub(o - 2)) for o in far]
    for copy in list_copies:
        copy.start()

    loads[3].wait()
    loads[4].wait()
    sep_copies[10].wait_recv()
    for l in range(NLEAF):
        leaf_load(l).wait()
        cm_load(l).wait()
        x = jnp.concatenate([lc[l], a1[...]], axis=1)
        acc[l] = mm(x, w[l, 0 : KL + B, :])

    for o in range(NOFF):
        for c in range(CLS):
            hit = one_hot(table[256 - SLOT // 2 : 256 + SLOT // 2], wanted[o][c : c + 1])
            pick[o, :, c * CW : (c + 1) * CW] = hit

    loads[2].wait()
    for n in range(7, 10):
        sep_copies[n].wait_recv()
    x23[:, 0:B] = jnp.transpose(a2[...])
    loads[1].wait()
    for n in range(7):
        sep_copies[n].wait_recv()
    x23[:, B : 2 * B] = jnp.transpose(a3[...])
    for l in range(NLEAF):
        both = acc[l] + mm(x23[...], w[l, KL + B : KL + 3 * B, :])
        disp[:, l * R : (l + 1) * R] = both.astype(BF16)

    def hot_rows(wish, into):
        for l in range(NLEAF):
            here = jnp.right_shift(wish, 9) == l
            v = jnp.where(here, jnp.bitwise_and(wish, R - 1) - 256, 999).astype(F32)
            into[l * R : (l + 1) * R, :] = one_hot(table[...], v)

    third = 3 - 2 * odd
    fourth = 4 - third

    def data_copy(r, target):
        return pltpu.make_async_remote_copy(
            src_ref=gath.at[r],
            dst_ref=got.at[r],
            send_sem=data_send.at[r],
            recv_sem=data_recv.at[r],
            device_id=(target, mo),
            device_id_type=MESH,
        )

    for copy in list_copies:
        copy.wait_recv()

    @pl.loop(0, 6)
    def _(t):
        late = t // 3
        part = lax.rem(t, 3)
        o1 = late * third
        o2 = 4 - o1
        r1, r2 = 3 * o1 + part, 3 * o2 + part
        hot_rows(jnp.concatenate([want[r1], want[r2]], axis=1), hot)
        both = mm(disp[...], hot[...]).astype(BF16)
        gath[r1] = both[:, 0:128]
        data_copy(r1, at_sub(2 - o1)).start()
        gath[r2] = both[:, 128:256]
        data_copy(r2, at_sub(2 - o2)).start()

    hot_rows(jnp.concatenate([lists[6], lists[7], lists[8]], axis=1), own_hot)
    own = mm(disp[...], own_hot[...]).astype(BF16)

    def arrived(o):
        for part in range(3):
            data_copy(3 * o + part, me).wait_recv()
        return [got[3 * o + part] for part in range(3)]

    x = jnp.concatenate([own] + arrived(third), axis=1)
    rhs = jnp.concatenate([pick[2], pick[third]], axis=0)
    cols32[...] = mm(x, rhs)
    x = jnp.concatenate(arrived(0) + arrived(4), axis=1)
    cols32[...] += mm(x, jnp.concatenate([pick[0], pick[4]], axis=0))
    for load in loads[5:]:
        load.wait()
    eye = lax.broadcasted_iota(jnp.int32, (MODES, MODES), 0) == lax.broadcasted_iota(
        jnp.int32, (MODES, MODES), 1
    )
    weight = jnp.sum(jnp.where(eye, mw[...], 0.0), axis=1, keepdims=True)
    x = jnp.concatenate(arrived(fourth), axis=1)
    cols[...] = (cols32[...] + mm(x, pick[fourth])).astype(BF16)
    out = pltpu.make_async_copy(cols, cols_h, in_sem.at[8])
    out.start()

    energies = []
    for c in range(CLS):
        s = mm(cols[:, c * CW : (c + 1) * CW], ops[c])
        e = jnp.sum(s * s * weight, axis=0, keepdims=True) * comp[c : c + 1]
        e = e[:, 0:128] + e[:, 128:256] + e[:, 256:384]
        energies.append((e + pltpu.roll(e, 64, 1)) * (0.5 / M))
    half = lax.broadcasted_iota(jnp.int32, (1, 128), 1) < 64
    terms[mo] = jnp.concatenate([jnp.where(half, energies[0], energies[1]), energies[2]], axis=1)
    en_copies = []
    for x in range(1, peers_mode):
        other = lax.rem(mo + x, peers_mode)
        copy = pltpu.make_async_remote_copy(
            src_ref=terms.at[mo],
            dst_ref=terms.at[mo],
            send_sem=en_send.at[x],
            recv_sem=en_recv.at[x],
            device_id=(me, other),
            device_id_type=MESH,
        )
        copy.start()
        en_copies.append(copy)

    for copy in sep_copies:
        copy.wait_send()
    for copy in list_copies:
        copy.wait_send()
    for o in far:
        for part in range(3):
            data_copy(3 * o + part, me).wait_send()
    for copy in en_copies:
        copy.wait_recv()
    total = terms[0]
    for x in range(1, peers_mode):
        total = total + terms[x]
    share = CLS * 64 // peers_mode
    total = pltpu.roll(total, lax.rem(256 - share * mo, 256), 1)
    energy[...] = total[:, 0:share]
    for copy in en_copies:
        copy.wait_send()
    out.wait()


def stress_kernel(cols_h, ops, sums_h, stress_h, energy_h, cols, stress, in_sem, out_sem):
    pass_on = pltpu.make_async_copy(sums_h, energy_h, out_sem.at[CLS])
    pass_on.start()
    loads = []
    for c in range(CLS):
        piece = pl.ds(c * CW, CW)
        loads.append(pltpu.make_async_copy(cols_h.at[:, piece], cols.at[:, piece], in_sem.at[c]))
        loads[c].start()
    stores = []
    for c in range(CLS):
        loads[c].wait()
        stress[c] = mm(cols[:, c * CW : (c + 1) * CW], ops[c])
        stores.append(pltpu.make_async_copy(stress.at[c], stress_h.at[c], out_sem.at[c]))
        stores[c].start()
    for store in stores:
        store.wait()
    pass_on.wait()


def shards(lc, lm, cm, s1, s2, s3, rows, ops, comp, mw):
    subs = lax.axis_size("sub")
    peers_mode = lax.axis_size("mode")
    share = CLS * 64 // peers_mode
    anywhere = pl.BlockSpec(memory_space=pl.ANY)
    vmem = pl.BlockSpec(memory_space=pltpu.VMEM)
    hbm = pl.BlockSpec(memory_space=pltpu.HBM)
    dma = pltpu.SemaphoreType.DMA
    cols, sums = pl.pallas_call(
        functools.partial(kernel, subs, peers_mode),
        out_shape=(
            jax.ShapeDtypeStruct((MODES, CLS * CW), BF16),
            jax.ShapeDtypeStruct((1, share), F32),
        ),
        in_specs=[anywhere] * 10,
        out_specs=(anywhere, vmem),
        scratch_shapes=[
            pltpu.VMEM((NLEAF, MODES, KL), BF16),
            pltpu.VMEM((NLEAF, KL + 3 * B, R), BF16),
            pltpu.VMEM((MODES, B), BF16),
            pltpu.VMEM((B, MODES), BF16),
            pltpu.VMEM((B, MODES), BF16),
            pltpu.VMEM((MODES, 2 * B), BF16),
            pltpu.VMEM((8, CW), jnp.int32),
            pltpu.VMEM((CLS, CW, SR), BF16),
            pltpu.VMEM((CLS, SR), F32),
            pltpu.VMEM((1, MODES), F32),
            pltpu.VMEM((NLEAF, MODES, R), F32),
            pltpu.VMEM((MODES, DOFS), BF16),
            pltpu.VMEM((R, 128), BF16),
            pltpu.VMEM((NOFF, SLOT, CLS * CW), BF16),
            pltpu.VMEM((3 * NOFF, 1, 128), jnp.int32),
            pltpu.VMEM((3 * NOFF, 1, 128), jnp.int32),
            pltpu.VMEM((DOFS, 256), BF16),
            pltpu.VMEM((DOFS, SLOT), BF16),
            pltpu.VMEM((3 * NOFF, MODES, 128), BF16),
            pltpu.VMEM((3 * NOFF, MODES, 128), BF16),
            pltpu.VMEM((MODES, CLS * CW), F32),
            pltpu.VMEM((MODES, CLS * CW), BF16),
            pltpu.VMEM((peers_mode, 1, 256), F32),
            dma((9,)),
            dma((NLEAF,)),
            dma((NLEAF,)),
            dma((11,)),
            dma((11,)),
            dma((NOFF,)),
            dma((NOFF,)),
            dma((3 * NOFF,)),
            dma((3 * NOFF,)),
            dma((4,)),
            dma((4,)),
        ],
        compiler_params=pltpu.CompilerParams(
            collective_id=0, has_side_effects=True, vmem_limit_bytes=40 * 2**20
        ),
        name="back_transform",
    )(
        lc,
        lm,
        cm.reshape(NLEAF, 3 * B, R),
        s1,
        s2.T,
        s3.T,
        rows,
        ops,
        comp,
        mw.reshape(1, MODES),
    )
    stress, energy = pl.pallas_call(
        stress_kernel,
        out_shape=(
            jax.ShapeDtypeStruct((CLS, MODES, SR), F32),
            jax.ShapeDtypeStruct((1, share), F32),
        ),
        in_specs=[hbm, vmem, hbm],
        out_specs=(anywhere, anywhere),
        scratch_shapes=[
            pltpu.VMEM((MODES, CLS * CW), BF16),
            pltpu.VMEM((CLS, MODES, SR), F32),
            dma((CLS,)),
            dma((CLS + 1,)),
        ],
        compiler_params=pltpu.CompilerParams(vmem_limit_bytes=16 * 2**20),
        name="stress_rows",
    )(cols, ops, sums)
    return stress, energy.reshape(share)


def solution(mesh):
    return jax.shard_map(
        shards,
        mesh=mesh,
        in_specs=(
            P("sub", "mode", None),
            P("sub", None, None),
            P("sub", None, None, None),
            P("mode", "sub"),
            P("mode", "sub"),
            P("mode", "sub"),
            P("sub", None),
            P("sub", None, None),
            P("sub", None),
            P("mode"),
        ),
        out_specs=(P("sub", "mode", None), P(("sub", "mode"))),
        check_vma=False,
    )
```

time: 41.7 us -> 49.6 us (1.19)
  the two profiles are of different devices: /device:TPU:8 before, /device:TPU:1 now
where the time goes in v2:
time: 49.6 us; the launch traced here: 49.1 us
  Pallas kernels  37.8 us (76%)
  local copies, waits for them, and re-layouts  10.6 us (21%)
  between operations  0.66 us (1%)
    pallas_call x1, Pallas kernels, shards(): pl.pallas_call(functools.partial(kernel, subs, peers_mode), out_shape=(ja...  36.2 us
    unnamed x20, local copies, waits for them, and re-layouts  10.6 us
    pallas_call x1, Pallas kernels, shards(): pl.pallas_call(stress_kernel, out_shape=(jax.ShapeDtypeStruct((CLS, MODES...  1.63 us

profile of v2, /device:TPU:1, one launch (start us, length us, event | category | flops | bytes accessed | tf_op | source)
XLA Modules:
  0.0 49.1 jit_solution(5656302566749423666)
XLA Ops:
  0.6 0.0 copy-start
  0.6 2.8 %copy-done = bf16[8,3,256,512]{3,2,1,0:T(8,128)(2,1)S(1)} copy-done((bf16[8,3,256,512]{3,2,1,0:T(8,128)(2,1)S(1)}, bf16[8,3,256,512]{3,2,1,0:T(8,128)(2,1)}, u32[]{:S(2)}) %copy-start) | copy-done | bytes 6291480
  3.4 0.0 copy-start.1
  3.4 1.3 %copy-done.1 = bf16[3,512,384]{2,1,0:T(8,128)(2,1)S(1)} copy-done((bf16[3,512,384]{2,1,0:T(8,128)(2,1)S(1)}, bf16[3,512,384]{2,1,0:T(8,128)(2,1)}, u32[]{:S(2)}) %copy-start.1) | copy-done | bytes 1179672
  4.7 0.0 copy-start.2
  4.7 1.2 %copy-done.2 = bf16[8,128,512]{2,1,0:T(8,128)(2,1)S(1)} copy-done((bf16[8,128,512]{2,1,0:T(8,128)(2,1)S(1)}, bf16[8,128,512]{2,1,0:T(8,128)(2,1)}, u32[]{:S(2)}) %copy-start.2) | copy-done | bytes 1048600
  5.9 0.0 copy-start.3
  5.9 1.0 %copy-done.3 = bf16[8,192,128]{2,1,0:T(8,128)(2,1)S(1)} copy-done((bf16[8,192,128]{2,1,0:T(8,128)(2,1)S(1)}, bf16[8,192,128]{2,1,0:T(8,128)(2,1)}, u32[]{:S(2)}) %copy-start.3) | copy-done | bytes 393240
  6.9 0.0 copy-start.4
  6.9 0.8 %copy-done.4 = bf16[192,128]{1,0:T(8,128)(2,1)S(1)} copy-done((bf16[192,128]{1,0:T(8,128)(2,1)S(1)}, bf16[192,128]{1,0:T(8,128)(2,1)}, u32[]{:S(2)}) %copy-start.4) | copy-done | bytes 49176
  7.7 0.0 copy-start.5
  7.7 0.8 %copy-done.5 = bf16[192,64]{0,1:T(8,128)(2,1)S(1)} copy-done((bf16[192,64]{0,1:T(8,128)(2,1)S(1)}, bf16[192,64]{0,1:T(8,128)(2,1)}, u32[]{:S(2)}) %copy-start.5) | copy-done | bytes 24600
  8.5 0.0 copy-start.6
  8.5 0.7 %copy-done.6 = bf16[192,32]{0,1:T(8,128)(2,1)S(1)} copy-done((bf16[192,32]{0,1:T(8,128)(2,1)S(1)}, bf16[192,32]{0,1:T(8,128)(2,1)}, u32[]{:S(2)}) %copy-start.6) | copy-done | bytes 12312
  9.2 0.0 copy-start.7
  9.2 0.7 %copy-done.7 = s32[3,512]{1,0:T(4,128)S(1)} copy-done((s32[3,512]{1,0:T(4,128)S(1)}, s32[3,512]{1,0:T(4,128)}, u32[]{:S(2)}) %copy-start.7) | copy-done | bytes 6168
  9.9 0.0 copy-start.8
  9.9 0.7 %copy-done.8 = f32[3,384]{1,0:T(4,128)S(1)} copy-done((f32[3,384]{1,0:T(4,128)S(1)}, f32[3,384]{1,0:T(4,128)}, u32[]{:S(2)}) %copy-start.8) | copy-done | bytes 4632
  10.6 0.0 copy-start.9
  10.6 0.7 %copy-done.9 = f32[192]{0:T(256)S(1)} copy-done((f32[192]{0:T(256)S(1)}, f32[192]{0:T(256)}, u32[]{:S(2)}) %copy-start.9) | copy-done | bytes 792
  11.3 36.2 %back_transform.1 = (bf16[192,1536]{1,0:T(8,128)(2,1)S(1)}, f32[1,48]{1,0:T(1,128)S(1)}) custom-call(bf16[8,192,128]{2,1,0:T(8,128)(2,1)S(1)} %copy-done.3, bf16[8,128,512]{2,1,0:T(8,128)(2,1)S(1)} %copy-done.2, bf16[8,768,512]{2,1,0:T(8,128)(2,1)S(1)} %bitcast.5, bf16[192,128]{1,0:T(8,128)(2,1)S(1)} %copy-done.4, bf16[64,192]{1,0:T(8,128)(2,1)S(1)} %bitcast.6, ...), custom_call_target="tpu_custom_call" | custom-call | tf_op jit(solution)/shard_map/back_transform/pallas_call | solution.py:365
  47.4 1.6 %stress_rows.1 = (f32[3,192,384]{2,1,0:T(8,128)}, f32[1,48]{1,0:T(1,128)}) custom-call(bf16[192,1536]{1,0:T(8,128)(2,1)S(1)} %get-tuple-element.6.cols_h, bf16[3,512,384]{2,1,0:T(8,128)(2,1)S(1)} %copy-done.1, f32[1,48]{1,0:T(1,128)S(1)} %get-tuple-element.7.sums_h), custom_call_target="tpu_custom_call" | custom-call | tf_op jit(solution)/shard_map/stress_rows/pallas_call | solution.py:425
Async XLA Ops:
  0.6 2.8 %copy-start = (bf16[8,3,256,512]{3,2,1,0:T(8,128)(2,1)S(1)}, bf16[8,3,256,512]{3,2,1,0:T(8,128)(2,1)}, u32[]{:S(2)}) copy-start(bf16[8,3,256,512]{3,2,1,0:T(8,128)(2,1)} %param.12) | copy-start | bytes 18874372
  3.4 1.3 %copy-start.1 = (bf16[3,512,384]{2,1,0:T(8,128)(2,1)S(1)}, bf16[3,512,384]{2,1,0:T(8,128)(2,1)}, u32[]{:S(2)}) copy-start(bf16[3,512,384]{2,1,0:T(8,128)(2,1)} %ops.1) | copy-start | bytes 3538948
  4.7 1.2 %copy-start.2 = (bf16[8,128,512]{2,1,0:T(8,128)(2,1)S(1)}, bf16[8,128,512]{2,1,0:T(8,128)(2,1)}, u32[]{:S(2)}) copy-start(bf16[8,128,512]{2,1,0:T(8,128)(2,1)} %lm_h.1) | copy-start | bytes 3145732
  5.9 1.0 %copy-start.3 = (bf16[8,192,128]{2,1,0:T(8,128)(2,1)S(1)}, bf16[8,192,128]{2,1,0:T(8,128)(2,1)}, u32[]{:S(2)}) copy-start(bf16[8,192,128]{2,1,0:T(8,128)(2,1)} %lc_h.1) | copy-start | bytes 1179652
  6.9 0.8 %copy-start.4 = (bf16[192,128]{1,0:T(8,128)(2,1)S(1)}, bf16[192,128]{1,0:T(8,128)(2,1)}, u32[]{:S(2)}) copy-start(bf16[192,128]{1,0:T(8,128)(2,1)} %s1_h.1) | copy-start | bytes 147460
  7.7 0.8 %copy-start.5 = (bf16[192,64]{0,1:T(8,128)(2,1)S(1)}, bf16[192,64]{0,1:T(8,128)(2,1)}, u32[]{:S(2)}) copy-start(bf16[192,64]{0,1:T(8,128)(2,1)} %param.14) | copy-start | bytes 73732
  8.5 0.7 %copy-start.6 = (bf16[192,32]{0,1:T(8,128)(2,1)S(1)}, bf16[192,32]{0,1:T(8,128)(2,1)}, u32[]{:S(2)}) copy-start(bf16[192,32]{0,1:T(8,128)(2,1)} %param.15) | copy-start | bytes 36868
  9.2 0.7 %copy-start.7 = (s32[3,512]{1,0:T(4,128)S(1)}, s32[3,512]{1,0:T(4,128)}, u32[]{:S(2)}) copy-start(s32[3,512]{1,0:T(4,128)} %rows_h.1) | copy-start | bytes 18436
  9.9 0.7 %copy-start.8 = (f32[3,384]{1,0:T(4,128)S(1)}, f32[3,384]{1,0:T(4,128)}, u32[]{:S(2)}) copy-start(f32[3,384]{1,0:T(4,128)} %comp_h.1) | copy-start | bytes 13828
  10.6 0.7 %copy-start.9 = (f32[192]{0:T(256)S(1)}, f32[192]{0:T(256)}, u32[]{:S(2)}) copy-start(f32[192]{0:T(256)} %param.19) | copy-start | bytes 2308

commit v3 on v2

--- a/solution.py
+++ b/solution.py
@@ -41,7 +41,7 @@
     ops_h,
     comp_h,
     mw_h,
-    cols_h,
+    stress,
     energy,
     lc,
     w,
@@ -121,9 +121,9 @@
         load.start()
     pl.semaphore_wait(barrier, greeted)
 
-    sends = [(s3_h, own3, n, x) for n, x in enumerate((7, 6, 5, 4, 3, 2, 1))]
+    sends = [(s1_h, own1, 10, 1)]
     sends += [(s2_h, own2, 7 + n, x) for n, x in enumerate((3, 2, 1))]
-    sends.append((s1_h, own1, 10, 1))
+    sends += [(s3_h, own3, n, x) for n, x in enumerate((7, 6, 5, 4, 3, 2, 1))]
     sep_copies = [
         pltpu.make_async_remote_copy(
             src_ref=src,
@@ -207,30 +207,27 @@
     for copy in list_copies:
         copy.start()
 
-    loads[3].wait()
-    loads[4].wait()
-    sep_copies[10].wait_recv()
-    for l in range(NLEAF):
-        leaf_load(l).wait()
-        cm_load(l).wait()
-        x = jnp.concatenate([lc[l], a1[...]], axis=1)
-        acc[l] = mm(x, w[l, 0 : KL + B, :])
-
     for o in range(NOFF):
         for c in range(CLS):
             hit = one_hot(table[256 - SLOT // 2 : 256 + SLOT // 2], wanted[o][c : c + 1])
             pick[o, :, c * CW : (c + 1) * CW] = hit
 
-    loads[2].wait()
-    for n in range(7, 10):
-        sep_copies[n].wait_recv()
+    for load in loads[2:5]:
+        load.wait()
+    for copy in sep_copies[0:4]:
+        copy.wait_recv()
     x23[:, 0:B] = jnp.transpose(a2[...])
+    for l in range(NLEAF):
+        leaf_load(l).wait()
+        cm_load(l).wait()
+        x = jnp.concatenate([lc[l], a1[...], x23[:, 0:B]], axis=1)
+        acc[l] = mm(x, w[l, 0 : KL + 2 * B, :])
     loads[1].wait()
-    for n in range(7):
-        sep_copies[n].wait_recv()
+    for copy in sep_copies[4:]:
+        copy.wait_recv()
     x23[:, B : 2 * B] = jnp.transpose(a3[...])
     for l in range(NLEAF):
-        both = acc[l] + mm(x23[...], w[l, KL + B : KL + 3 * B, :])
+        both = acc[l] + mm(x23[:, B : 2 * B], w[l, KL + 2 * B : KL + 3 * B, :])
         disp[:, l * R : (l + 1) * R] = both.astype(BF16)
 
     def hot_rows(wish, into):
@@ -290,12 +287,10 @@
     weight = jnp.sum(jnp.where(eye, mw[...], 0.0), axis=1, keepdims=True)
     x = jnp.concatenate(arrived(fourth), axis=1)
     cols[...] = (cols32[...] + mm(x, pick[fourth])).astype(BF16)
-    out = pltpu.make_async_copy(cols, cols_h, in_sem.at[8])
-    out.start()
-
     energies = []
     for c in range(CLS):
         s = mm(cols[:, c * CW : (c + 1) * CW], ops[c])
+        stress[c] = s
         e = jnp.sum(s * s * weight, axis=0, keepdims=True) * comp[c : c + 1]
         e = e[:, 0:128] + e[:, 128:256] + e[:, 256:384]
         energies.append((e + pltpu.roll(e, 64, 1)) * (0.5 / M))
@@ -332,26 +327,16 @@
     energy[...] = total[:, 0:share]
     for copy in en_copies:
         copy.wait_send()
-    out.wait()
-
-
-def stress_kernel(cols_h, ops, sums_h, stress_h, energy_h, cols, stress, in_sem, out_sem):
-    pass_on = pltpu.make_async_copy(sums_h, energy_h, out_sem.at[CLS])
-    pass_on.start()
-    loads = []
+
+
+def hand_out(stress_v, energy_v, stress_h, energy_h, sem):
+    copies = [pltpu.make_async_copy(energy_v, energy_h, sem.at[CLS])]
     for c in range(CLS):
-        piece = pl.ds(c * CW, CW)
-        loads.append(pltpu.make_async_copy(cols_h.at[:, piece], cols.at[:, piece], in_sem.at[c]))
-        loads[c].start()
-    stores = []
-    for c in range(CLS):
-        loads[c].wait()
-        stress[c] = mm(cols[:, c * CW : (c + 1) * CW], ops[c])
-        stores.append(pltpu.make_async_copy(stress.at[c], stress_h.at[c], out_sem.at[c]))
-        stores[c].start()
-    for store in stores:
-        store.wait()
-    pass_on.wait()
+        copies.append(pltpu.make_async_copy(stress_v.at[c], stress_h.at[c], sem.at[c]))
+    for copy in copies:
+        copy.start()
+    for copy in copies:
+        copy.wait()
 
 
 def shards(lc, lm, cm, s1, s2, s3, rows, ops, comp, mw):
@@ -360,16 +345,27 @@
     share = CLS * 64 // peers_mode
     anywhere = pl.BlockSpec(memory_space=pl.ANY)
     vmem = pl.BlockSpec(memory_space=pltpu.VMEM)
-    hbm = pl.BlockSpec(memory_space=pltpu.HBM)
     dma = pltpu.SemaphoreType.DMA
-    cols, sums = pl.pallas_call(
+    values = (
+        lc,
+        lm,
+        cm.reshape(NLEAF, 3 * B, R),
+        s1,
+        s2.T,
+        s3.T,
+        rows,
+        ops,
+        comp,
+        mw.reshape(1, MODES),
+    )
+    stress, energy = pl.pallas_call(
         functools.partial(kernel, subs, peers_mode),
         out_shape=(
-            jax.ShapeDtypeStruct((MODES, CLS * CW), BF16),
-            jax.ShapeDtypeStruct((1, share), F32),
+            pltpu.VMEM((CLS, MODES, SR), F32),
+            pltpu.VMEM((1, share), F32),
         ),
         in_specs=[anywhere] * 10,
-        out_specs=(anywhere, vmem),
+        out_specs=(vmem, vmem),
         scratch_shapes=[
             pltpu.VMEM((NLEAF, MODES, KL), BF16),
             pltpu.VMEM((NLEAF, KL + 3 * B, R), BF16),
@@ -394,7 +390,7 @@
             pltpu.VMEM((MODES, CLS * CW), F32),
             pltpu.VMEM((MODES, CLS * CW), BF16),
             pltpu.VMEM((peers_mode, 1, 256), F32),
-            dma((9,)),
+            dma((8,)),
             dma((NLEAF,)),
             dma((NLEAF,)),
             dma((11,)),
@@ -407,38 +403,22 @@
             dma((4,)),
         ],
         compiler_params=pltpu.CompilerParams(
-            collective_id=0, has_side_effects=True, vmem_limit_bytes=40 * 2**20
+            collective_id=0, has_side_effects=True, vmem_limit_bytes=44 * 2**20
         ),
         name="back_transform",
-    )(
-        lc,
-        lm,
-        cm.reshape(NLEAF, 3 * B, R),
-        s1,
-        s2.T,
-        s3.T,
-        rows,
-        ops,
-        comp,
-        mw.reshape(1, MODES),
-    )
+    )(*[pltpu.with_memory_space_constraint(value, pltpu.HBM) for value in values])
     stress, energy = pl.pallas_call(
-        stress_kernel,
+        hand_out,
         out_shape=(
             jax.ShapeDtypeStruct((CLS, MODES, SR), F32),
             jax.ShapeDtypeStruct((1, share), F32),
         ),
-        in_specs=[hbm, vmem, hbm],
+        in_specs=[anywhere] * 2,
         out_specs=(anywhere, anywhere),
-        scratch_shapes=[
-            pltpu.VMEM((MODES, CLS * CW), BF16),
-            pltpu.VMEM((CLS, MODES, SR), F32),
-            dma((CLS,)),
-            dma((CLS + 1,)),
-        ],
+        scratch_shapes=[dma((CLS + 1,))],
         compiler_params=pltpu.CompilerParams(vmem_limit_bytes=16 * 2**20),
-        name="stress_rows",
-    )(cols, ops, sums)
+        name="hand_out",
+    )(stress, energy)
     return stress, energy.reshape(share)
 
 

time: 49.6 us -> 36.3 us (0.73)
  the two profiles are of different devices: /device:TPU:1 before, /device:TPU:6 now
where the time goes in v3:
time: 36.3 us; the launch traced here: 36 us
  Pallas kernels  35.4 us (98%)
  between operations  0.64 us (2%)
    pallas_call x1, Pallas kernels, shards(): pl.pallas_call(functools.partial(kernel, subs, peers_mode), out_shape=(pl...  34.4 us
    pallas_call x1, Pallas kernels, shards(): pl.pallas_call(hand_out, out_shape=(jax.ShapeDtypeStruct((CLS, MODES, SR)...  0.95 us

profile of v3, /device:TPU:6, one launch (start us, length us, event | category | flops | bytes accessed | tf_op | source)
XLA Modules:
  0.0 36.0 jit_solution(664301131851351666)
XLA Ops:
  0.6 34.4 %back_transform.1 = (f32[3,192,384]{2,1,0:T(8,128)S(1)}, f32[1,48]{1,0:T(1,128)S(1)}) custom-call(bf16[8,192,128]{2,1,0:T(8,128)(2,1)} %lc_h.1, bf16[8,128,512]{2,1,0:T(8,128)(2,1)} %lm_h.1, bf16[8,768,512]{2,1,0:T(8,128)(2,1)} %bitcast.5, bf16[192,128]{1,0:T(8,128)(2,1)} %s1_h.1, bf16[64,192]{1,0:T(8,128)(2,1)} %bitcast.6, bf16[32,192]{1,0:T(8,128)(2,1)} %bitcast.7, ...), custom_call_target="tpu_custom_call" | custom-call | tf_op jit(solution)/shard_map/back_transform/pallas_call | solution.py:361
  35.1 0.9 %hand_out.1 = (f32[3,192,384]{2,1,0:T(8,128)}, f32[1,48]{1,0:T(1,128)}) custom-call(f32[3,192,384]{2,1,0:T(8,128)S(1)} %get-tuple-element.6.stress_v, f32[1,48]{1,0:T(1,128)S(1)} %get-tuple-element.7.energy_v), custom_call_target="tpu_custom_call" | custom-call | tf_op jit(solution)/shard_map/hand_out/pallas_call | solution.py:410

commit v4 on v3

--- a/solution.py
+++ b/solution.py
@@ -119,25 +119,6 @@
     ]
     for load in loads[:4]:
         load.start()
-    pl.semaphore_wait(barrier, greeted)
-
-    sends = [(s1_h, own1, 10, 1)]
-    sends += [(s2_h, own2, 7 + n, x) for n, x in enumerate((3, 2, 1))]
-    sends += [(s3_h, own3, n, x) for n, x in enumerate((7, 6, 5, 4, 3, 2, 1))]
-    sep_copies = [
-        pltpu.make_async_remote_copy(
-            src_ref=src,
-            dst_ref=dst,
-            send_sem=sep_send.at[n],
-            recv_sem=sep_recv.at[n],
-            device_id=(in_group(x), mo),
-            device_id_type=MESH,
-        )
-        for src, dst, n, x in sends
-    ]
-    for copy in sep_copies:
-        copy.start()
-
     def leaf_load(l):
         return pltpu.make_async_copy(lm_h.at[l], w.at[l, pl.ds(0, KL), :], leaf_sem.at[l])
 
@@ -150,6 +131,41 @@
         cm_load(l).start()
     for load in loads[5:]:
         load.start()
+
+    pl.semaphore_wait(barrier, greeted)
+
+    chip, chip_of_two = in_eight // 2, in_four // 2
+    sibling = in_group(1)
+
+    def core_one(x):
+        return me - in_eight + 2 * jnp.bitwise_xor(chip, x) + 1
+
+    def sep_copy(src, dst, sent, landed, target):
+        return pltpu.make_async_remote_copy(
+            src_ref=src,
+            dst_ref=dst,
+            send_sem=sep_send.at[sent],
+            recv_sem=sep_recv.at[landed],
+            device_id=(target, mo),
+            device_id_type=MESH,
+        )
+
+    sep_copies = [
+        sep_copy(s2_h, own2, 0, 6 + odd, core_one(1)),
+        sep_copy(s3_h, own3, 1, odd, core_one(1)),
+        sep_copy(s3_h, own3, 2, 2 + odd, core_one(2)),
+        sep_copy(s3_h, own3, 3, 4 + odd, core_one(3)),
+        sep_copy(s1_h, own1, 4, 10, sibling),
+        sep_copy(s2_h, own2, 5, 9, sibling),
+        sep_copy(s3_h, own3, 6, 8, sibling),
+    ]
+    for copy in sep_copies:
+        copy.start()
+    other_two = a2.at[pl.ds(pl.multiple_of(128 * (1 - chip_of_two), 128), 128), :]
+    pass_on = [sep_copy(other_two, other_two, 7, 11, sibling)]
+    for x in (1, 2, 3):
+        rows_of = pl.ds(pl.multiple_of(64 * jnp.bitwise_xor(chip, x), 64), 64)
+        pass_on.append(sep_copy(a3.at[rows_of, :], a3.at[rows_of, :], 7 + x, 11 + x, sibling))
 
     table[...] = (lax.broadcasted_iota(jnp.int32, (R, 128), 0) - 256).astype(F32).astype(BF16)
     earlier = (
@@ -212,22 +228,39 @@
             hit = one_hot(table[256 - SLOT // 2 : 256 + SLOT // 2], wanted[o][c : c + 1])
             pick[o, :, c * CW : (c + 1) * CW] = hit
 
-    for load in loads[2:5]:
-        load.wait()
-    for copy in sep_copies[0:4]:
-        copy.wait_recv()
-    x23[:, 0:B] = jnp.transpose(a2[...])
+    loads[3].wait()
+    loads[4].wait()
+    sep_copies[4].wait_recv()
     for l in range(NLEAF):
         leaf_load(l).wait()
         cm_load(l).wait()
-        x = jnp.concatenate([lc[l], a1[...], x23[:, 0:B]], axis=1)
-        acc[l] = mm(x, w[l, 0 : KL + 2 * B, :])
-    loads[1].wait()
-    for copy in sep_copies[4:]:
+        x = jnp.concatenate([lc[l], a1[...]], axis=1)
+        acc[l] = mm(x, w[l, 0 : KL + B, :])
+
+    for load in loads[1:3]:
+        load.wait()
+    for copy in sep_copies[5:]:
         copy.wait_recv()
+
+    @pl.when(odd == 1)
+    def _():
+        for k in range(2):
+            sep_copy(s2_h, own2, 0, 6 + k, sibling).wait_recv()
+        pass_on[0].start()
+        for x in (1, 2, 3):
+            for k in range(2):
+                sep_copy(s3_h, own3, x, 2 * (x - 1) + k, sibling).wait_recv()
+            pass_on[x].start()
+
+    @pl.when(odd == 0)
+    def _():
+        for copy in pass_on:
+            copy.wait_recv()
+
+    x23[:, 0:B] = jnp.transpose(a2[...])
     x23[:, B : 2 * B] = jnp.transpose(a3[...])
     for l in range(NLEAF):
-        both = acc[l] + mm(x23[:, B : 2 * B], w[l, KL + 2 * B : KL + 3 * B, :])
+        both = acc[l] + mm(x23[...], w[l, KL + B : KL + 3 * B, :])
         disp[:, l * R : (l + 1) * R] = both.astype(BF16)
 
     def hot_rows(wish, into):
@@ -312,6 +345,12 @@
 
     for copy in sep_copies:
         copy.wait_send()
+
+    @pl.when(odd == 1)
+    def _():
+        for copy in pass_on:
+            copy.wait_send()
+
     for copy in list_copies:
         copy.wait_send()
     for o in far:
@@ -394,7 +433,7 @@
             dma((NLEAF,)),
             dma((NLEAF,)),
             dma((11,)),
-            dma((11,)),
+            dma((15,)),
             dma((NOFF,)),
             dma((NOFF,)),
             dma((3 * NOFF,)),

time: 36.3 us -> 35.1 us (0.967)
  Pallas kernels: 35.4 us -> 34.3 us
    pallas_call x1, Pallas kernels: 34.4 us -> 33.4 us  [shards(): pl.pallas_call(functools.partial(kernel, subs, peers_mode), out_shape=(pl...]
where the time goes in v4:
time: 35.1 us; the launch traced here: 35 us
  Pallas kernels  34.3 us (98%)
  between operations  0.64 us (2%)
    pallas_call x1, Pallas kernels, shards(): pl.pallas_call(functools.partial(kernel, subs, peers_mode), out_shape=(pl...  33.4 us
    pallas_call x1, Pallas kernels, shards(): pl.pallas_call(hand_out, out_shape=(jax.ShapeDtypeStruct((CLS, MODES, SR)...  0.95 us

profile of v4, /device:TPU:6, one launch (start us, length us, event | category | flops | bytes accessed | tf_op | source)
XLA Modules:
  0.0 35.0 jit_solution(1987243195489107575)
XLA Ops:
  0.6 33.4 %back_transform.1 = (f32[3,192,384]{2,1,0:T(8,128)S(1)}, f32[1,48]{1,0:T(1,128)S(1)}) custom-call(bf16[8,192,128]{2,1,0:T(8,128)(2,1)} %lc_h.1, bf16[8,128,512]{2,1,0:T(8,128)(2,1)} %lm_h.1, bf16[8,768,512]{2,1,0:T(8,128)(2,1)} %bitcast.5, bf16[192,128]{1,0:T(8,128)(2,1)} %s1_h.1, bf16[64,192]{1,0:T(8,128)(2,1)} %bitcast.6, bf16[32,192]{1,0:T(8,128)(2,1)} %bitcast.7, ...), custom_call_target="tpu_custom_call" | custom-call | tf_op jit(solution)/shard_map/back_transform/pallas_call | solution.py:400
  34.0 0.9 %hand_out.1 = (f32[3,192,384]{2,1,0:T(8,128)}, f32[1,48]{1,0:T(1,128)}) custom-call(f32[3,192,384]{2,1,0:T(8,128)S(1)} %get-tuple-element.6.stress_v, f32[1,48]{1,0:T(1,128)S(1)} %get-tuple-element.7.energy_v), custom_call_target="tpu_custom_call" | custom-call | tf_op jit(solution)/shard_map/hand_out/pallas_call | solution.py:449

commit v5 on v4

--- a/solution.py
+++ b/solution.py
@@ -132,41 +132,6 @@
     for load in loads[5:]:
         load.start()
 
-    pl.semaphore_wait(barrier, greeted)
-
-    chip, chip_of_two = in_eight // 2, in_four // 2
-    sibling = in_group(1)
-
-    def core_one(x):
-        return me - in_eight + 2 * jnp.bitwise_xor(chip, x) + 1
-
-    def sep_copy(src, dst, sent, landed, target):
-        return pltpu.make_async_remote_copy(
-            src_ref=src,
-            dst_ref=dst,
-            send_sem=sep_send.at[sent],
-            recv_sem=sep_recv.at[landed],
-            device_id=(target, mo),
-            device_id_type=MESH,
-        )
-
-    sep_copies = [
-        sep_copy(s2_h, own2, 0, 6 + odd, core_one(1)),
-        sep_copy(s3_h, own3, 1, odd, core_one(1)),
-        sep_copy(s3_h, own3, 2, 2 + odd, core_one(2)),
-        sep_copy(s3_h, own3, 3, 4 + odd, core_one(3)),
-        sep_copy(s1_h, own1, 4, 10, sibling),
-        sep_copy(s2_h, own2, 5, 9, sibling),
-        sep_copy(s3_h, own3, 6, 8, sibling),
-    ]
-    for copy in sep_copies:
-        copy.start()
-    other_two = a2.at[pl.ds(pl.multiple_of(128 * (1 - chip_of_two), 128), 128), :]
-    pass_on = [sep_copy(other_two, other_two, 7, 11, sibling)]
-    for x in (1, 2, 3):
-        rows_of = pl.ds(pl.multiple_of(64 * jnp.bitwise_xor(chip, x), 64), 64)
-        pass_on.append(sep_copy(a3.at[rows_of, :], a3.at[rows_of, :], 7 + x, 11 + x, sibling))
-
     table[...] = (lax.broadcasted_iota(jnp.int32, (R, 128), 0) - 256).astype(F32).astype(BF16)
     earlier = (
         lax.broadcasted_iota(jnp.int32, (CW, CW), 0) < lax.broadcasted_iota(jnp.int32, (CW, CW), 1)
@@ -208,6 +173,41 @@
     for r in range(3 * NOFF):
         lists[r] = found[r : r + 1]
 
+    pl.semaphore_wait(barrier, greeted)
+
+    chip, chip_of_two = in_eight // 2, in_four // 2
+    sibling = in_group(1)
+
+    def core_one(x):
+        return me - in_eight + 2 * jnp.bitwise_xor(chip, x) + 1
+
+    def sep_copy(src, dst, sent, landed, target):
+        return pltpu.make_async_remote_copy(
+            src_ref=src,
+            dst_ref=dst,
+            send_sem=sep_send.at[sent],
+            recv_sem=sep_recv.at[landed],
+            device_id=(target, mo),
+            device_id_type=MESH,
+        )
+
+    sep_copies = [
+        sep_copy(s2_h, own2, 0, 6 + odd, core_one(1)),
+        sep_copy(s3_h, own3, 1, odd, core_one(1)),
+        sep_copy(s3_h, own3, 2, 2 + odd, core_one(2)),
+        sep_copy(s3_h, own3, 3, 4 + odd, core_one(3)),
+        sep_copy(s1_h, own1, 4, 10, sibling),
+        sep_copy(s2_h, own2, 5, 9, sibling),
+        sep_copy(s3_h, own3, 6, 8, sibling),
+    ]
+    for n in (4, 1, 2, 3, 0, 5, 6):
+        sep_copies[n].start()
+    other_two = a2.at[pl.ds(pl.multiple_of(128 * (1 - chip_of_two), 128), 128), :]
+    pass_on = [sep_copy(other_two, other_two, 7, 11, sibling)]
+    for x in (1, 2, 3):
+        rows_of = pl.ds(pl.multiple_of(64 * jnp.bitwise_xor(chip, x), 64), 64)
+        pass_on.append(sep_copy(a3.at[rows_of, :], a3.at[rows_of, :], 7 + x, 11 + x, sibling))
+
     def list_copy(o, target):
         return pltpu.make_async_remote_copy(
             src_ref=lists.at[pl.ds(3 * o, 3)],
@@ -330,7 +330,7 @@
     half = lax.broadcasted_iota(jnp.int32, (1, 128), 1) < 64
     terms[mo] = jnp.concatenate([jnp.where(half, energies[0], energies[1]), energies[2]], axis=1)
     en_copies = []
-    for x in range(1, peers_mode):
+    for x in (2, 1, 3):
         other = lax.rem(mo + x, peers_mode)
         copy = pltpu.make_async_remote_copy(
             src_ref=terms.at[mo],

time: 35.1 us -> 35.2 us (level); the launches traced: 35 us -> 34.7 us
  no operation moved by 1% of the time
where the time goes in v5:
time: 35.2 us; the launch traced here: 34.7 us
  Pallas kernels  34 us (97%)
  between operations  0.64 us (2%)
    pallas_call x1, Pallas kernels, shards(): pl.pallas_call(functools.partial(kernel, subs, peers_mode), out_shape=(pl...  33.1 us
    pallas_call x1, Pallas kernels, shards(): pl.pallas_call(hand_out, out_shape=(jax.ShapeDtypeStruct((CLS, MODES, SR)...  0.95 us

profile of v5, /device:TPU:6, one launch (start us, length us, event | category | flops | bytes accessed | tf_op | source)
XLA Modules:
  0.0 34.7 jit_solution(4123982458100800493)
XLA Ops:
  0.6 33.1 %back_transform.1 = (f32[3,192,384]{2,1,0:T(8,128)S(1)}, f32[1,48]{1,0:T(1,128)S(1)}) custom-call(bf16[8,192,128]{2,1,0:T(8,128)(2,1)} %lc_h.1, bf16[8,128,512]{2,1,0:T(8,128)(2,1)} %lm_h.1, bf16[8,768,512]{2,1,0:T(8,128)(2,1)} %bitcast.5, bf16[192,128]{1,0:T(8,128)(2,1)} %s1_h.1, bf16[64,192]{1,0:T(8,128)(2,1)} %bitcast.6, bf16[32,192]{1,0:T(8,128)(2,1)} %bitcast.7, ...), custom_call_target="tpu_custom_call" | custom-call | tf_op jit(solution)/shard_map/back_transform/pallas_call | solution.py:400
  33.7 0.9 %hand_out.1 = (f32[3,192,384]{2,1,0:T(8,128)}, f32[1,48]{1,0:T(1,128)}) custom-call(f32[3,192,384]{2,1,0:T(8,128)S(1)} %get-tuple-element.6.stress_v, f32[1,48]{1,0:T(1,128)S(1)} %get-tuple-element.7.energy_v), custom_call_target="tpu_custom_call" | custom-call | tf_op jit(solution)/shard_map/hand_out/pallas_call | solution.py:449
